TPU v7x, 768 devices: a whole 4x8x12 slice. The times are simulated.
768 devices in a mesh: ri: 12 (over z), ao: 64 (over x, y, core).
Axes of the slice: x: 4, y: 8, z: 12, core: 2. Of those that a mesh axis runs over, the one named last changes fastest.
Arguments:
- three_center: bfloat16 [12, 512, 512, 256], P('ri', None, 'ao'), may hold values from -0.375 to 0.375
- occ_density: bfloat16 [12, 512, 512], P('ri'), may hold values from -0.25 to 0.25
- virt_density: bfloat16 [12, 512, 512], P('ri'), may hold values from -0.25 to 0.25
- pair_mask: int32 [12, 16, 16], P('ri'), may hold values 0 or 1
- occ_mask: int32 [12, 16, 16], P('ri'), may hold values 0 or 1
- virt_mask: int32 [12, 16, 16], P('ri'), may hold values 0 or 1
Outputs:
- response: float32 [256, 256], P('ao')
All inputs are finite; a program needn't handle non-finite values. No bound on the sum of `pair_mask` or of `occ_mask` or of `virt_mask` on one device may be relied on, other than what follows from the above.
Results may differ from a plain program's by a relative error of at most 0.0041.
Values may be sent and summed in bfloat16 or wider, within the bound.
A program may use at most 32 MiB of HBM per device.

v0:
```python
import jax
import jax.numpy as jnp
from jax import lax
from jax.sharding import PartitionSpec as P


def broadcast_pairs(mask, block_width):
    full = jnp.repeat(jnp.repeat(mask, block_width, axis=0), block_width, axis=1)
    return full.astype(jnp.bfloat16)


def body(three_center, occ_density, virt_density, pair_mask, occ_mask, virt_mask):
    three_index_tensor = three_center[0]
    total_orb = three_index_tensor.shape[0]
    own_cols = three_index_tensor.shape[1]
    block_width = total_orb // pair_mask.shape[1]
    column_start = lax.axis_index("ao") * own_cols
    pair_full = broadcast_pairs(pair_mask[0], block_width)
    pair_cols = lax.dynamic_slice_in_dim(pair_full, column_start, own_cols, 1)
    masked = three_index_tensor * pair_cols[:, :, None]
    occ_m = occ_density[0] * broadcast_pairs(occ_mask[0], block_width)
    virtual_masked = virt_density[0] * broadcast_pairs(virt_mask[0], block_width)
    first = jnp.einsum("lm,mnp->lnp", occ_m, masked, preferred_element_type=jnp.float32).astype(
        jnp.bfloat16
    )
    regrouped = lax.all_to_all(first, "ao", split_axis=0, concat_axis=1, tiled=True)
    second = jnp.einsum(
        "lnp,ns->lsp", regrouped, virtual_masked, preferred_element_type=jnp.float32
    ).astype(jnp.bfloat16)
    partial_sum = jnp.einsum("lsp,slq->pq", second, masked, preferred_element_type=jnp.float32)
    summed = lax.psum(partial_sum, "ri")
    return lax.psum_scatter(summed, "ao", scatter_dimension=0, tiled=True)


def solution(mesh):
    return jax.shard_map(
        body,
        mesh=mesh,
        in_specs=(
            P("ri", None, "ao", None),
            P("ri", None, None),
            P("ri", None, None),
            P("ri", None, None),
            P("ri", None, None),
            P("ri", None, None),
        ),
        out_specs=P("ao", None),
        check_vma=False,
    )
```

profile of v0, /device:TPU:6, one launch (start us, length us, event | category | flops | bytes accessed | tf_op | source)
XLA Modules:
  0.0 312.4 jit_solution(11530700326158133257)
XLA Ops:
  6.5 0.0 copy-start
  6.5 0.8 convert_bitcast_fusion
  7.4 0.1 copy.36
  7.5 0.1 broadcast_in_dim.23
  7.6 0.1 convert_element_type.75
  7.8 0.2 copy.37
  7.9 1.3 copy.35
  9.2 0.7 convert_bitcast_fusion.1
  9.9 0.1 copy.34
  10.0 0.1 broadcast_in_dim.21
  10.1 0.1 convert_element_type.71
  10.2 0.0 copy-done
  10.2 0.7 multiply_bitcast_fusion
  11.0 1.3 fusion.9
  12.3 2.5 copy.40
  14.8 0.0 copy-start.1
  14.8 14.9 %all-to-all-start = ((bf16[512,8,256]{2,1,0:T(8,128)(2,1)}), bf16[512,8,256]{2,1,0:T(8,128)(2,1)}, u32[]{:S(2)}, u32[]{:S(2)}) async-start(bf16[512,8,256]{2,1,0:T(8,128)(2,1)} %copy.40), calls=%async_computation | async-start | bytes 4194304 | tf_op jit(solution)/shard_map/all_to_all | solution.py:26
  29.7 0.0 all-reduce.3.cloned.1.call-start
  29.7 0.0 copy-done.1
  29.7 0.2 copy.33
  29.9 0.0 copy-done.2
  30.0 0.1 copy.32
  30.1 0.1 broadcast_in_dim.19
  30.2 0.1 convert_element_type.67
  30.3 1.7 bitcast_multiply_fusion
  32.0 46.5 %all-to-all-done = bf16[512,8,256]{2,1,0:T(8,128)(2,1)} async-done(((bf16[512,8,256]{2,1,0:T(8,128)(2,1)}), bf16[512,8,256]{2,1,0:T(8,128)(2,1)}, u32[]{:S(2)}, u32[]{:S(2)}) %all-to-all-start) | async-done | bytes 2097184 | tf_op jit(solution)/shard_map/all_to_all | solution.py:26
  78.5 4.9 %fusion.16 = f32[256,256]{1,0:T(8,128)} fusion(bf16[512,8,256]{2,1,0:T(8,128)(2,1)} %bitcast_multiply_fusion, bf16[8,64,8,256]{3,2,0,1:T(8,128)(2,1)} %bitcast.12, bf16[1,512,512]{1,2,0:T(8,128)(2,1)S(1)} %bitcast_multiply_fusion.2), kind=kOutput, calls=%fused_computation.12 | convolution fusion | flops 1611661312 | bytes 4980736 | tf_op jit(solution)/shard_map/lsp,slq->pq/dot_general | solution.py:30
  83.5 0.0 all-reduce.3.cloned.1.call-update
  83.5 1.3 dynamic-slice
  85.4 194.2 %all-reduce.3.cloned.1.call-done = f32[256,256]{1,0:T(8,128)} async-done(((f32[256,256]{1,0:T(8,128)}), f32[256,256]{1,0:T(8,128)}) %all-reduce.3.cloned.1.call-update) | async-done | bytes 262160
  279.6 0.7 constant_dynamic-slice_fusion
  280.3 25.3 %psum.8 = f32[4,256]{1,0:T(4,128)} all-reduce(f32[4,256]{1,0:T(4,128)S(1)} %constant_dynamic-slice_fusion), channel_id=1, replica_groups=mesh['ri'=12,'ao'=64] {'ri'}, use_global_device_ids=true, to_apply=%region_0.0 | all-reduce | flops 1024 | bytes 8192 | tf_op jit(solution)/shard_map/psum | solution.py:31
  (6 shorter events, 0.1 us)
Async XLA Ops:
  6.5 3.7 %copy-start = (bf16[1,512,8,256]{3,2,1,0:T(8,128)(2,1)S(1)}, bf16[1,512,8,256]{3,2,1,0:T(8,128)(2,1)}, u32[]{:S(2)}) copy-start(bf16[1,512,8,256]{3,2,1,0:T(8,128)(2,1)} %param.6) | copy-start | bytes 6291460
  14.8 14.9 %copy-start.1 = (bf16[1,512,512]{2,1,0:T(8,128)(2,1)S(1)}, bf16[1,512,512]{2,1,0:T(8,128)(2,1)}, u32[]{:S(2)}) copy-start(bf16[1,512,512]{2,1,0:T(8,128)(2,1)} %param.8) | copy-start | bytes 1572868
  14.8 15.2 %copy-start.2 = (s32[1,16,16]{2,1,0:T(8,128)S(1)}, s32[1,16,16]{2,1,0:T(8,128)}, u32[]{:S(2)}) copy-start(s32[1,16,16]{2,1,0:T(8,128)} %param.11) | copy-start | bytes 3076
  14.8 63.7 %all-to-all-start = ((bf16[512,8,256]{2,1,0:T(8,128)(2,1)}), bf16[512,8,256]{2,1,0:T(8,128)(2,1)}, u32[]{:S(2)}, u32[]{:S(2)}) async-start(bf16[512,8,256]{2,1,0:T(8,128)(2,1)} %copy.40), calls=%async_computation | async-start | bytes 4194304 | tf_op jit(solution)/shard_map/all_to_all | solution.py:26
  29.7 249.9 %all-reduce.3.cloned.1.call-start = ((), (), s32[]{:S(2)}) async-start(), calls=%async_computation.1 | async-start | bytes 524288
Sparse Core Ops, SparseCore 0:
  83.6 195.9 all-reduce.2
where the time goes:
time: 314 us; the launch traced here: 312 us
  waiting for transfers between devices  241 us (77%)
  blocking collectives  25.3 us (8%)
  starting transfers between devices  14.9 us (5%)
  between operations  14.2 us (5%)
  local copies, waits for them, and re-layouts  7.09 us (2%)
  matrix products  6.23 us (2%)
  other arithmetic  4.03 us (1%)
    unnamed x2, waiting for transfers between devices  194 us
    all_to_all x1, waiting for transfers between devices, body(): lax.all_to_all(first, 'ao', split_axis=0, concat_axis=1, tiled=True)  46.5 us
    psum x1, blocking collectives, body(): summed = lax.psum(partial_sum, 'ri')  25.3 us
    all_to_all x1, starting transfers between devices, body(): lax.all_to_all(first, 'ao', split_axis=0, concat_axis=1, tiled=True)  14.9 us
  transfers between devices with their start and end apart: 2, of which 2 were waited for; matrix products, arithmetic and copies ran while one was open for 1% of the time, Pallas kernels for 0%

commit v1 on v0

v1 whole, which is shorter than its diff:
```python
import functools

import jax
import jax.numpy as jnp
from jax import lax
from jax.experimental import pallas as pl
from jax.experimental.pallas import tpu as pltpu
from jax.sharding import PartitionSpec as P

MESH = pl.DeviceIdType.MESH
X, Y, C, Z = 4, 8, 2, 12
AO = X * Y * C
NA, NP, W, BLOCKS = 512, 256, 8, 16
HALF = 128
SLABS = NP // HALF
F32, BF16 = jnp.float32, jnp.bfloat16


def dot(a, b, ca=1, cb=0):
    return lax.dot_general(a, b, (((ca,), (cb,)), ((), ())), preferred_element_type=F32)


def masked_density(density, mask, own_row):
    spread = (
        lax.broadcasted_iota(jnp.int32, (NA, BLOCKS), 0) // (NA // BLOCKS)
        == lax.broadcasted_iota(jnp.int32, (NA, BLOCKS), 1)
    ).astype(F32).astype(BF16)
    flags = (mask.astype(F32) * own_row).astype(BF16)
    rows = dot(spread, flags).astype(BF16)
    return density * dot(rows, spread, 1, 1).astype(BF16)


def kernel(
    three_hbm, occ_hbm, virt_hbm, pair_ref, occ_mask_ref, virt_mask_ref, out_ref,
    three, occ, virt, flat, cols, snd, rcv, tall, wide, psnd, prcv, zsnd, zrcv,
    load_sem, ssem, rsem, psend_sem, psem, zsend_sem, zsem,
):
    me = lax.axis_index("ao")
    z = lax.axis_index("ri")
    x, y, c = me // (Y * C), (me // C) % Y, me % C

    loads = [
        pltpu.make_async_copy(three_hbm.at[0, :, :, pl.ds(0, HALF)], three.at[0], load_sem.at[0]),
        pltpu.make_async_copy(occ_hbm.at[0], occ, load_sem.at[2]),
        pltpu.make_async_copy(three_hbm.at[0, :, :, pl.ds(HALF, HALF)], three.at[1], load_sem.at[1]),
        pltpu.make_async_copy(virt_hbm.at[0], virt, load_sem.at[3]),
    ]
    for load in loads:
        load.start()

    barrier = pltpu.get_barrier_semaphore()

    def greet(k, _):
        pl.semaphore_signal(barrier, inc=1, device_id={"ao": lax.rem(me + k, AO)}, device_id_type=MESH)
        return 0

    def greet_z(k, _):
        pl.semaphore_signal(barrier, inc=1, device_id={"ri": lax.rem(z + k, Z)}, device_id_type=MESH)
        return 0

    lax.fori_loop(1, AO, greet, 0)
    lax.fori_loop(1, Z, greet_z, 0)

    own = (lax.broadcasted_iota(jnp.int32, (8, BLOCKS), 1) == me // (NA // BLOCKS // W)).astype(F32).astype(BF16)
    own_row = dot(own, pair_ref[0].astype(F32).astype(BF16), 1, 1)[0:1]

    loads[1].wait()
    occ[...] = masked_density(occ[...], occ_mask_ref[0], own_row)

    for h in range(SLABS):
        loads[2 * h].wait()
        flat[...] = three[h].astype(F32).reshape(NA * W, HALF)
        for k in range(W // 2):
            even = flat[pl.ds(2 * k, NA, stride=W), :]
            odd = flat[pl.ds(2 * k + 1, NA, stride=W), :]
            cols[h, k] = jnp.concatenate([even, odd], axis=1).astype(BF16)
            first = dot(occ[...], cols[h, k])
            pair = [first[:, i * HALF : (i + 1) * HALF].reshape(AO, W, HALF) for i in range(2)]
            snd[h, :, 2 * W * k : 2 * W * (k + 1), :] = jnp.concatenate(pair, axis=1).astype(BF16)

        if h == 0:
            pl.semaphore_wait(barrier, AO - 1 + Z - 1)

        place = x * C + c
        pltpu.make_async_copy(snd.at[h, me], rcv.at[h, y, place], rsem.at[h, 0]).start()

        def send(k, _):
            dy = (k // C) % Y
            tx, ty, tc = lax.rem(x + k // (Y * C), X), lax.rem(y + dy, Y), lax.rem(c + k, C)
            target = (tx * Y + ty) * C + tc
            pltpu.make_async_remote_copy(
                src_ref=snd.at[h, target],
                dst_ref=rcv.at[h, y, place],
                send_sem=ssem.at[h],
                recv_sem=rsem.at[h, dy],
                device_id={"ao": target},
                device_id_type=MESH,
            ).start()
            return 0

        lax.fori_loop(1, AO, send, 0)

    loads[3].wait()
    virt[...] = masked_density(virt[...], virt_mask_ref[0], own_row)
    for h in range(SLABS):
        for k in range(W // 2):
            other = dot(virt[...], cols[h, k])
            for i in range(2):
                tall[h, pl.ds(2 * k + i, NA, stride=W), :] = other[:, i * HALF : (i + 1) * HALF]

    def turn(ty, _):
        for h in range(SLABS):
            for tx in range(X):
                rows = pl.multiple_of((tx * Y + ty) * (C * W * W), C * W * W)
                block = tall[h, pl.ds(rows, C * W * W), :]
                wide[ty, h * HALF : (h + 1) * HALF, tx * C * W * W : (tx + 1) * C * W * W] = block.T.astype(BF16)
        return 0

    lax.fori_loop(0, Y, turn, 0)

    def window_sum():
        pltpu.make_async_copy(prcv, prcv, psem).wait()
        zsnd[...] = jnp.sum(prcv[...], axis=0)
        zrcv[z] = zsnd[...]

        def send(k, _):
            pltpu.make_async_remote_copy(
                src_ref=zsnd,
                dst_ref=zrcv.at[z],
                send_sem=zsend_sem,
                recv_sem=zsem,
                device_id={"ri": lax.rem(z + k, Z)},
                device_id_type=MESH,
            ).start()
            return 0

        lax.fori_loop(1, Z, send, 0)

    for h in range(SLABS):
        total = jnp.zeros((NP, HALF), F32)
        for step, dy in enumerate((0, 1, 7, 2, 6, 3, 5, 4)):
            sy = lax.rem(y + Y - dy, Y)
            pltpu.make_async_copy(rcv.at[h, sy], rcv.at[h, sy], rsem.at[h, dy]).wait()
            total += dot(wide[sy], rcv[h, sy].reshape(X * C * W * W, HALF))
            if h == 1 and step == 4:
                pl.when(x < X // 2)(window_sum)
        low = total[:HALF].T.reshape(AO // 4, 8, HALF)
        high = total[HALF:].T.reshape(AO // 4, 8, HALF)
        top = lax.broadcasted_iota(jnp.int32, low.shape, 1) < 4
        psnd[h, :, 0] = jnp.where(top, low, pltpu.roll(high, 4, 1))
        psnd[h, :, 1] = jnp.where(top, pltpu.roll(low, 4, 1), high)

        def send(k, _):
            rank = lax.rem(me + k, AO // 2)
            target = h * (AO // 2) + rank

            @pl.when(target == me)
            def _():
                pltpu.make_async_copy(psnd.at[h, rank // C, rank % C], prcv.at[me], psem).start()

            @pl.when(target != me)
            def _():
                pltpu.make_async_remote_copy(
                    src_ref=psnd.at[h, rank // C, rank % C],
                    dst_ref=prcv.at[me],
                    send_sem=psend_sem,
                    recv_sem=psem,
                    device_id={"ao": target},
                    device_id_type=MESH,
                ).start()

            return 0

        lax.fori_loop(0, AO // 2, send, 0)

    pl.when(x >= X // 2)(window_sum)
    pltpu.make_async_copy(zrcv.at[pl.ds(0, Z - 1)], zrcv.at[pl.ds(0, Z - 1)], zsem).wait()
    total = jnp.sum(zrcv[...], axis=0)
    out_ref[:, 0:HALF] = total[0:4]
    out_ref[:, HALF:NP] = total[4:8]

    for h in range(SLABS):
        pltpu.make_async_copy(snd.at[h, pl.ds(0, AO - 1)], snd.at[h, pl.ds(0, AO - 1)], ssem.at[h]).wait()
    pltpu.make_async_copy(prcv.at[pl.ds(0, AO - 1)], prcv.at[pl.ds(0, AO - 1)], psend_sem).wait()
    pltpu.make_async_copy(zrcv.at[pl.ds(0, Z - 1)], zrcv.at[pl.ds(0, Z - 1)], zsend_sem).wait()


def body(three_center, occ_density, virt_density, pair_mask, occ_mask, virt_mask):
    hbm = pl.BlockSpec(memory_space=pl.ANY)
    vmem = pl.BlockSpec(memory_space=pltpu.VMEM)
    dma = pltpu.SemaphoreType.DMA
    return pl.pallas_call(
        kernel,
        out_shape=jax.ShapeDtypeStruct((NP // AO, NP), F32),
        in_specs=[hbm, hbm, hbm, vmem, vmem, vmem],
        out_specs=vmem,
        scratch_shapes=[
            pltpu.VMEM((SLABS, NA, W, HALF), BF16),
            pltpu.VMEM((NA, NA), BF16),
            pltpu.VMEM((NA, NA), BF16),
            pltpu.VMEM((NA * W, HALF), F32),
            pltpu.VMEM((SLABS, W // 2, NA, 2 * HALF), BF16),
            pltpu.VMEM((SLABS, AO, W * W, HALF), BF16),
            pltpu.VMEM((SLABS, Y, X * C, W * W, HALF), BF16),
            pltpu.VMEM((SLABS, NA * W, HALF), F32),
            pltpu.VMEM((Y, NP, X * C * W * W), BF16),
            pltpu.VMEM((SLABS, AO // 4, C, 8, HALF), F32),
            pltpu.VMEM((AO, 8, HALF), F32),
            pltpu.VMEM((8, HALF), F32),
            pltpu.VMEM((Z, 8, HALF), F32),
            dma((4,)), dma((SLABS,)), dma((SLABS, Y)), dma, dma, dma, dma,
        ],
        compiler_params=pltpu.CompilerParams(
            collective_id=0, has_side_effects=True, vmem_limit_bytes=40 * 2**20
        ),
        name="response",
    )(three_center, occ_density, virt_density, pair_mask, occ_mask, virt_mask)


def solution(mesh):
    return jax.shard_map(
        body,
        mesh=mesh,
        in_specs=(
            P("ri", None, "ao", None),
            P("ri", None, None),
            P("ri", None, None),
            P("ri", None, None),
            P("ri", None, None),
            P("ri", None, None),
        ),
        out_specs=P("ao", None),
        check_vma=False,
    )
```

time: 314 us -> 92.2 us (0.29)
  waiting for transfers between devices: 241 us -> 0 us
  Pallas kernels: 0 us -> 85.4 us
  blocking collectives: 25.3 us -> 0 us
  starting transfers between devices: 14.9 us -> 0 us
  between operations: 14.2 us -> 0.02 us
  matrix products: 6.23 us -> 0 us
  other arithmetic: 4.03 us -> 0 us
    unnamed x2 -> x0, waiting for transfers between devices: 194 us -> none
    pallas_call x0 -> x1, Pallas kernels: none -> 85.4 us  [body(): pl.pallas_call(kernel, out_shape=jax.ShapeDtypeStruct((NP // AO, NP), F32...]
    all_to_all x1 -> x0, waiting for transfers between devices: 46.5 us -> none  [body(): lax.all_to_all(first, 'ao', split_axis=0, concat_axis=1, tiled=True)]
    psum x1 -> x0, blocking collectives: 25.3 us -> none  [body(): summed = lax.psum(partial_sum, 'ri')]
    all_to_all x1 -> x0, starting transfers between devices: 14.9 us -> none  [body(): lax.all_to_all(first, 'ao', split_axis=0, concat_axis=1, tiled=True)]
    dot_general x2 -> x0, matrix products: 6.23 us -> none  [the longest x1 4.94 us: body(): jnp.einsum('lsp,slq->pq', second, masked, preferred_element_type=jnp.floa...]
    unnamed x10 -> x13, local copies, waits for them, and re-layouts: 3.46 us -> 6.36 us
  transfers between devices with their start and end apart: 2 -> 0, of which waited for: 2 -> 0; matrix products, arithmetic and copies ran while one was open for 1% -> 0% of each run, Pallas kernels for 0% -> 0%
where the time goes in v1:
time: 92.2 us; the launch traced here: 91.8 us
  Pallas kernels  85.4 us (93%)
  local copies, waits for them, and re-layouts  6.36 us (7%)
    pallas_call x1, Pallas kernels, body(): pl.pallas_call(kernel, out_shape=jax.ShapeDtypeStruct((NP // AO, NP), F32...  85.4 us
    unnamed x13, local copies, waits for them, and re-layouts  6.36 us

profile of v1, /device:TPU:6, one launch (start us, length us, event | category | flops | bytes accessed | tf_op | source)
XLA Modules:
  0.0 91.8 jit_solution(15582633316220058626)
XLA Ops:
  0.0 0.0 copy-start
  0.0 1.6 %copy-done = bf16[1,512,8,256]{3,2,1,0:T(8,128)(2,1)S(1)} copy-done((bf16[1,512,8,256]{3,2,1,0:T(8,128)(2,1)S(1)}, bf16[1,512,8,256]{3,2,1,0:T(8,128)(2,1)}, u32[]{:S(2)}) %copy-start) | copy-done | bytes 2097176
  1.6 0.0 copy-start.1
  1.6 1.0 %copy-done.1 = bf16[1,512,512]{2,1,0:T(8,128)(2,1)S(1)} copy-done((bf16[1,512,512]{2,1,0:T(8,128)(2,1)S(1)}, bf16[1,512,512]{2,1,0:T(8,128)(2,1)}, u32[]{:S(2)}) %copy-start.1) | copy-done | bytes 524312
  2.6 0.0 copy-start.2
  2.6 1.0 %copy-done.2 = bf16[1,512,512]{2,1,0:T(8,128)(2,1)S(1)} copy-done((bf16[1,512,512]{2,1,0:T(8,128)(2,1)S(1)}, bf16[1,512,512]{2,1,0:T(8,128)(2,1)}, u32[]{:S(2)}) %copy-start.2) | copy-done | bytes 524312
  3.7 0.0 copy-start.3
  3.7 0.7 copy-done.3
  4.4 0.0 copy-start.4
  4.4 0.7 copy-done.4
  5.1 0.0 copy-start.5
  5.1 0.7 copy-done.5
  5.8 85.4 %response.1 = f32[4,256]{1,0:T(4,128)S(1)} custom-call(bf16[1,512,8,256]{3,2,1,0:T(8,128)(2,1)S(1)} %copy-done, bf16[1,512,512]{2,1,0:T(8,128)(2,1)S(1)} %copy-done.1, bf16[1,512,512]{2,1,0:T(8,128)(2,1)S(1)} %copy-done.2, s32[1,16,16]{2,1,0:T(8,128)S(1)} %copy-done.3, s32[1,16,16]{2,1,0:T(8,128)S(1)} %copy-done.4, s32[1,16,16]{2,1,0:T(8,128)S(1)} %copy-done.5), custom_call_target="tpu_custom_call" | custom-call | tf_op jit(solution)/shard_map/response/pallas_call | solution.py:192
  91.2 0.6 copy.8
Async XLA Ops:
  0.0 1.6 %copy-start = (bf16[1,512,8,256]{3,2,1,0:T(8,128)(2,1)S(1)}, bf16[1,512,8,256]{3,2,1,0:T(8,128)(2,1)}, u32[]{:S(2)}) copy-start(bf16[1,512,8,256]{3,2,1,0:T(8,128)(2,1)} %three_hbm.1) | copy-start | bytes 6291460
  1.6 1.0 %copy-start.1 = (bf16[1,512,512]{2,1,0:T(8,128)(2,1)S(1)}, bf16[1,512,512]{2,1,0:T(8,128)(2,1)}, u32[]{:S(2)}) copy-start(bf16[1,512,512]{2,1,0:T(8,128)(2,1)} %occ_hbm.1) | copy-start | bytes 1572868
  2.6 1.0 %copy-start.2 = (bf16[1,512,512]{2,1,0:T(8,128)(2,1)S(1)}, bf16[1,512,512]{2,1,0:T(8,128)(2,1)}, u32[]{:S(2)}) copy-start(bf16[1,512,512]{2,1,0:T(8,128)(2,1)} %virt_hbm.1) | copy-start | bytes 1572868
  3.7 0.7 copy-start.3
  4.4 0.7 copy-start.4
  5.1 0.7 copy-start.5

commit v2 on v1

--- a/solution.py
+++ b/solution.py
@@ -10,9 +10,13 @@
 MESH = pl.DeviceIdType.MESH
 X, Y, C, Z = 4, 8, 2, 12
 AO = X * Y * C
+CHIPS = X * Y
+EARLY_SEND, EARLY_SUM = 5, -1
 NA, NP, W, BLOCKS = 512, 256, 8, 16
 HALF = 128
 SLABS = NP // HALF
+FAR_Y = (4, 3, 5, 2, 6, 1, 7, 0)
+FAR_Z = (6, 5, 7, 4, 8, 3, 9, 2, 10, 1, 11)
 F32, BF16 = jnp.float32, jnp.bfloat16
 
 
@@ -31,15 +35,18 @@
 
 
 def kernel(
-    three_hbm, occ_hbm, virt_hbm, pair_ref, occ_mask_ref, virt_mask_ref, out_ref,
-    three, occ, virt, flat, cols, snd, rcv, tall, wide, psnd, prcv, zsnd, zrcv,
-    load_sem, ssem, rsem, psend_sem, psem, zsend_sem, zsem,
+    three_hbm, occ_hbm, virt_hbm, pair_hbm, occ_mask_hbm, virt_mask_hbm, out_ref,
+    masks, three, occ, virt, flat, cols, snd, rcv, tall, wide, psnd, pmate, psum, prcv, zsnd, zrcv,
+    load_sem, ssem, rsem, mate_send, mate_sem, psend_sem, psem, zsend_sem, zsem,
 ):
     me = lax.axis_index("ao")
     z = lax.axis_index("ri")
     x, y, c = me // (Y * C), (me // C) % Y, me % C
 
     loads = [
+        pltpu.make_async_copy(pair_hbm, masks.at[pl.ds(0, 1)], load_sem.at[4]),
+        pltpu.make_async_copy(occ_mask_hbm, masks.at[pl.ds(1, 1)], load_sem.at[5]),
+        pltpu.make_async_copy(virt_mask_hbm, masks.at[pl.ds(2, 1)], load_sem.at[6]),
         pltpu.make_async_copy(three_hbm.at[0, :, :, pl.ds(0, HALF)], three.at[0], load_sem.at[0]),
         pltpu.make_async_copy(occ_hbm.at[0], occ, load_sem.at[2]),
         pltpu.make_async_copy(three_hbm.at[0, :, :, pl.ds(HALF, HALF)], three.at[1], load_sem.at[1]),
@@ -50,25 +57,27 @@
 
     barrier = pltpu.get_barrier_semaphore()
 
-    def greet(k, _):
-        pl.semaphore_signal(barrier, inc=1, device_id={"ao": lax.rem(me + k, AO)}, device_id_type=MESH)
-        return 0
-
-    def greet_z(k, _):
-        pl.semaphore_signal(barrier, inc=1, device_id={"ri": lax.rem(z + k, Z)}, device_id_type=MESH)
-        return 0
-
-    lax.fori_loop(1, AO, greet, 0)
-    lax.fori_loop(1, Z, greet_z, 0)
+    for dz in FAR_Z:
+        pl.semaphore_signal(barrier, inc=1, device_id={"ri": lax.rem(z + dz, Z)}, device_id_type=MESH)
+    for dy in FAR_Y:
+
+        def greet(k, _):
+            target = (lax.rem(x + k // C, X) * Y + lax.rem(y + dy, Y)) * C + lax.rem(c + k, C)
+            pl.semaphore_signal(barrier, inc=1, device_id={"ao": target}, device_id_type=MESH)
+            return 0
+
+        lax.fori_loop(int(dy == 0), X * C, greet, 0)
 
     own = (lax.broadcasted_iota(jnp.int32, (8, BLOCKS), 1) == me // (NA // BLOCKS // W)).astype(F32).astype(BF16)
-    own_row = dot(own, pair_ref[0].astype(F32).astype(BF16), 1, 1)[0:1]
-
-    loads[1].wait()
-    occ[...] = masked_density(occ[...], occ_mask_ref[0], own_row)
-
-    for h in range(SLABS):
-        loads[2 * h].wait()
+    for load in loads[:3]:
+        load.wait()
+    own_row = dot(own, masks[0].astype(F32).astype(BF16), 1, 1)[0:1]
+
+    loads[4].wait()
+    occ[...] = masked_density(occ[...], masks[1], own_row)
+
+    for h in range(SLABS):
+        loads[3 + 2 * h].wait()
         flat[...] = three[h].astype(F32).reshape(NA * W, HALF)
         for k in range(W // 2):
             even = flat[pl.ds(2 * k, NA, stride=W), :]
@@ -100,8 +109,8 @@
 
         lax.fori_loop(1, AO, send, 0)
 
-    loads[3].wait()
-    virt[...] = masked_density(virt[...], virt_mask_ref[0], own_row)
+    loads[6].wait()
+    virt[...] = masked_density(virt[...], masks[2], own_row)
     for h in range(SLABS):
         for k in range(W // 2):
             other = dot(virt[...], cols[h, k])
@@ -118,62 +127,78 @@
 
     lax.fori_loop(0, Y, turn, 0)
 
+    chip = x * Y + y
+
+    def chip_sum(h):
+        part = pl.ds(h * CHIPS // SLABS, CHIPS // SLABS)
+        copy = pltpu.make_async_remote_copy(
+            src_ref=psnd.at[1 - c, part],
+            dst_ref=pmate.at[part],
+            send_sem=mate_send.at[h],
+            recv_sem=mate_sem.at[h],
+            device_id={"ao": me + 1 - 2 * c},
+            device_id_type=MESH,
+        )
+        copy.start()
+        copy.wait_recv()
+        psum[part] = psnd[c, part] + pmate[part]
+        return copy
+
+    def plane_send(h):
+        for dy in FAR_Y:
+            for tx in range(h * X // SLABS, (h + 1) * X // SLABS):
+                target = tx * Y + lax.rem(y + dy, Y)
+
+                @pl.when(target != chip)
+                def _():
+                    pltpu.make_async_remote_copy(
+                        src_ref=psum.at[target],
+                        dst_ref=prcv.at[chip],
+                        send_sem=psend_sem,
+                        recv_sem=psem,
+                        device_id={"ao": C * target + c},
+                        device_id_type=MESH,
+                    ).start()
+
     def window_sum():
-        pltpu.make_async_copy(prcv, prcv, psem).wait()
+        prcv[chip] = psum[chip]
+        pltpu.make_async_copy(prcv.at[pl.ds(0, CHIPS - 1)], prcv.at[pl.ds(0, CHIPS - 1)], psem).wait()
         zsnd[...] = jnp.sum(prcv[...], axis=0)
         zrcv[z] = zsnd[...]
-
-        def send(k, _):
+        for dz in FAR_Z:
             pltpu.make_async_remote_copy(
                 src_ref=zsnd,
                 dst_ref=zrcv.at[z],
                 send_sem=zsend_sem,
                 recv_sem=zsem,
-                device_id={"ri": lax.rem(z + k, Z)},
+                device_id={"ri": lax.rem(z + dz, Z)},
                 device_id_type=MESH,
             ).start()
-            return 0
-
-        lax.fori_loop(1, Z, send, 0)
-
+
+    mates = []
     for h in range(SLABS):
         total = jnp.zeros((NP, HALF), F32)
         for step, dy in enumerate((0, 1, 7, 2, 6, 3, 5, 4)):
             sy = lax.rem(y + Y - dy, Y)
             pltpu.make_async_copy(rcv.at[h, sy], rcv.at[h, sy], rsem.at[h, dy]).wait()
             total += dot(wide[sy], rcv[h, sy].reshape(X * C * W * W, HALF))
-            if h == 1 and step == 4:
+            if h == 1 and step == EARLY_SEND:
+                plane_send(0)
+            if h == 1 and step == EARLY_SUM:
                 pl.when(x < X // 2)(window_sum)
-        low = total[:HALF].T.reshape(AO // 4, 8, HALF)
-        high = total[HALF:].T.reshape(AO // 4, 8, HALF)
+        low = total[:HALF].T.reshape(CHIPS // SLABS, 8, HALF)
+        high = total[HALF:].T.reshape(CHIPS // SLABS, 8, HALF)
         top = lax.broadcasted_iota(jnp.int32, low.shape, 1) < 4
-        psnd[h, :, 0] = jnp.where(top, low, pltpu.roll(high, 4, 1))
-        psnd[h, :, 1] = jnp.where(top, pltpu.roll(low, 4, 1), high)
-
-        def send(k, _):
-            rank = lax.rem(me + k, AO // 2)
-            target = h * (AO // 2) + rank
-
-            @pl.when(target == me)
-            def _():
-                pltpu.make_async_copy(psnd.at[h, rank // C, rank % C], prcv.at[me], psem).start()
-
-            @pl.when(target != me)
-            def _():
-                pltpu.make_async_remote_copy(
-                    src_ref=psnd.at[h, rank // C, rank % C],
-                    dst_ref=prcv.at[me],
-                    send_sem=psend_sem,
-                    recv_sem=psem,
-                    device_id={"ao": target},
-                    device_id_type=MESH,
-                ).start()
-
-            return 0
-
-        lax.fori_loop(0, AO // 2, send, 0)
-
-    pl.when(x >= X // 2)(window_sum)
+        part = pl.ds(h * CHIPS // SLABS, CHIPS // SLABS)
+        psnd[0, part] = jnp.where(top, low, pltpu.roll(high, 4, 1))
+        psnd[1, part] = jnp.where(top, pltpu.roll(low, 4, 1), high)
+        mates.append(chip_sum(h))
+
+    plane_send(1)
+    if EARLY_SUM < 0:
+        window_sum()
+    else:
+        pl.when(x >= X // 2)(window_sum)
     pltpu.make_async_copy(zrcv.at[pl.ds(0, Z - 1)], zrcv.at[pl.ds(0, Z - 1)], zsem).wait()
     total = jnp.sum(zrcv[...], axis=0)
     out_ref[:, 0:HALF] = total[0:4]
@@ -181,7 +206,9 @@
 
     for h in range(SLABS):
         pltpu.make_async_copy(snd.at[h, pl.ds(0, AO - 1)], snd.at[h, pl.ds(0, AO - 1)], ssem.at[h]).wait()
-    pltpu.make_async_copy(prcv.at[pl.ds(0, AO - 1)], prcv.at[pl.ds(0, AO - 1)], psend_sem).wait()
+    for mate in mates:
+        mate.wait_send()
+    pltpu.make_async_copy(prcv.at[pl.ds(0, CHIPS - 1)], prcv.at[pl.ds(0, CHIPS - 1)], psend_sem).wait()
     pltpu.make_async_copy(zrcv.at[pl.ds(0, Z - 1)], zrcv.at[pl.ds(0, Z - 1)], zsend_sem).wait()
 
 
@@ -192,9 +219,10 @@
     return pl.pallas_call(
         kernel,
         out_shape=jax.ShapeDtypeStruct((NP // AO, NP), F32),
-        in_specs=[hbm, hbm, hbm, vmem, vmem, vmem],
+        in_specs=[hbm] * 6,
         out_specs=vmem,
         scratch_shapes=[
+            pltpu.VMEM((3, BLOCKS, BLOCKS), jnp.int32),
             pltpu.VMEM((SLABS, NA, W, HALF), BF16),
             pltpu.VMEM((NA, NA), BF16),
             pltpu.VMEM((NA, NA), BF16),
@@ -204,14 +232,16 @@
             pltpu.VMEM((SLABS, Y, X * C, W * W, HALF), BF16),
             pltpu.VMEM((SLABS, NA * W, HALF), F32),
             pltpu.VMEM((Y, NP, X * C * W * W), BF16),
-            pltpu.VMEM((SLABS, AO // 4, C, 8, HALF), F32),
-            pltpu.VMEM((AO, 8, HALF), F32),
+            pltpu.VMEM((C, CHIPS, 8, HALF), F32),
+            pltpu.VMEM((CHIPS, 8, HALF), F32),
+            pltpu.VMEM((CHIPS, 8, HALF), F32),
+            pltpu.VMEM((CHIPS, 8, HALF), F32),
             pltpu.VMEM((8, HALF), F32),
             pltpu.VMEM((Z, 8, HALF), F32),
-            dma((4,)), dma((SLABS,)), dma((SLABS, Y)), dma, dma, dma, dma,
+            dma((7,)), dma((SLABS,)), dma((SLABS, Y)), dma((SLABS,)), dma((SLABS,)), dma, dma, dma, dma,
         ],
         compiler_params=pltpu.CompilerParams(
-            collective_id=0, has_side_effects=True, vmem_limit_bytes=40 * 2**20
+            collective_id=0, has_side_effects=True, vmem_limit_bytes=60 * 2**20
         ),
         name="response",
     )(three_center, occ_density, virt_density, pair_mask, occ_mask, virt_mask)

time: 92.2 us -> 81.7 us (0.89)
  Pallas kernels: 85.4 us -> 80.2 us
  local copies, waits for them, and re-layouts: 6.36 us -> 1.28 us
    pallas_call x1, Pallas kernels: 85.4 us -> 80.2 us  [body(): pl.pallas_call(kernel, out_shape=jax.ShapeDtypeStruct((NP // AO, NP), F32...]
    unnamed x13 -> x1, local copies, waits for them, and re-layouts: 6.36 us -> 1.28 us
where the time goes in v2:
time: 81.7 us; the launch traced here: 81.5 us
  Pallas kernels  80.2 us (98%)
  local copies, waits for them, and re-layouts  1.28 us (2%)
    pallas_call x1, Pallas kernels, body(): pl.pallas_call(kernel, out_shape=jax.ShapeDtypeStruct((NP // AO, NP), F32...  80.2 us

profile of v2, /device:TPU:6, one launch (start us, length us, event | category | flops | bytes accessed | tf_op | source)
XLA Modules:
  0.0 81.5 jit_solution(6000198541630951820)
XLA Ops:
  0.0 80.2 %response.1 = f32[4,256]{1,0:T(4,128)} custom-call(bf16[1,512,8,256]{3,2,1,0:T(8,128)(2,1)} %three_hbm.1, bf16[1,512,512]{2,1,0:T(8,128)(2,1)} %occ_hbm.1, bf16[1,512,512]{2,1,0:T(8,128)(2,1)} %virt_hbm.1, s32[1,16,16]{2,1,0:T(8,128)} %pair_hbm.1, s32[1,16,16]{2,1,0:T(8,128)} %occ_mask_hbm.1, s32[1,16,16]{2,1,0:T(8,128)} %virt_mask_hbm.1), custom_call_target="tpu_custom_call" | custom-call | tf_op jit(solution)/shard_map/response/pallas_call | solution.py:219
  80.2 1.3 %copy.8 = f32[4,256]{1,0:T(4,128)} copy(f32[4,256]{1,0:T(4,128)} %response.1) | data formatting | bytes 8192

commit v3 on v2

--- a/solution.py
+++ b/solution.py
@@ -11,12 +11,14 @@
 X, Y, C, Z = 4, 8, 2, 12
 AO = X * Y * C
 CHIPS = X * Y
-EARLY_SEND, EARLY_SUM = 5, -1
+EARLY_SEND = 6
 NA, NP, W, BLOCKS = 512, 256, 8, 16
 HALF = 128
 SLABS = NP // HALF
 FAR_Y = (4, 3, 5, 2, 6, 1, 7, 0)
 FAR_Z = (6, 5, 7, 4, 8, 3, 9, 2, 10, 1, 11)
+PAIR_Y = (4, 1, 7, 2, 6, 3, 5, 0)
+SETS = ((0, 0), (0, 1), (1, 0), (1, 1), (3, 0), (3, 1), (2, 0), (2, 1))
 F32, BF16 = jnp.float32, jnp.bfloat16
 
 
@@ -42,6 +44,19 @@
     me = lax.axis_index("ao")
     z = lax.axis_index("ri")
     x, y, c = me // (Y * C), (me // C) % Y, me % C
+
+    barrier = pltpu.get_barrier_semaphore()
+
+    for dz in FAR_Z:
+        pl.semaphore_signal(barrier, inc=1, device_id={"ri": lax.rem(z + dz, Z)}, device_id_type=MESH)
+    for dy in FAR_Y:
+
+        def greet(k, _):
+            target = (lax.rem(x + k // C, X) * Y + lax.rem(y + dy, Y)) * C + lax.rem(c + k, C)
+            pl.semaphore_signal(barrier, inc=1, device_id={"ao": target}, device_id_type=MESH)
+            return 0
+
+        lax.fori_loop(int(dy == 0), X * C, greet, 0)
 
     loads = [
         pltpu.make_async_copy(pair_hbm, masks.at[pl.ds(0, 1)], load_sem.at[4]),
@@ -55,19 +70,6 @@
     for load in loads:
         load.start()
 
-    barrier = pltpu.get_barrier_semaphore()
-
-    for dz in FAR_Z:
-        pl.semaphore_signal(barrier, inc=1, device_id={"ri": lax.rem(z + dz, Z)}, device_id_type=MESH)
-    for dy in FAR_Y:
-
-        def greet(k, _):
-            target = (lax.rem(x + k // C, X) * Y + lax.rem(y + dy, Y)) * C + lax.rem(c + k, C)
-            pl.semaphore_signal(barrier, inc=1, device_id={"ao": target}, device_id_type=MESH)
-            return 0
-
-        lax.fori_loop(int(dy == 0), X * C, greet, 0)
-
     own = (lax.broadcasted_iota(jnp.int32, (8, BLOCKS), 1) == me // (NA // BLOCKS // W)).astype(F32).astype(BF16)
     for load in loads[:3]:
         load.wait()
@@ -90,24 +92,20 @@
         if h == 0:
             pl.semaphore_wait(barrier, AO - 1 + Z - 1)
 
-        place = x * C + c
-        pltpu.make_async_copy(snd.at[h, me], rcv.at[h, y, place], rsem.at[h, 0]).start()
-
-        def send(k, _):
-            dy = (k // C) % Y
-            tx, ty, tc = lax.rem(x + k // (Y * C), X), lax.rem(y + dy, Y), lax.rem(c + k, C)
-            target = (tx * Y + ty) * C + tc
-            pltpu.make_async_remote_copy(
-                src_ref=snd.at[h, target],
-                dst_ref=rcv.at[h, y, place],
-                send_sem=ssem.at[h],
-                recv_sem=rsem.at[h, dy],
-                device_id={"ao": target},
-                device_id_type=MESH,
-            ).start()
-            return 0
-
-        lax.fori_loop(1, AO, send, 0)
+        own_set = x * C + c
+        pltpu.make_async_copy(snd.at[h, me], rcv.at[h, own_set, y], rsem.at[h, 0]).start()
+        for g, (dx, dc) in enumerate(SETS):
+            for dy in PAIR_Y:
+                if dx or dc or dy:
+                    target = (lax.rem(x + dx, X) * Y + lax.rem(y + dy, Y)) * C + lax.rem(c + dc, C)
+                    pltpu.make_async_remote_copy(
+                        src_ref=snd.at[h, target],
+                        dst_ref=rcv.at[h, own_set, y],
+                        send_sem=ssem.at[h],
+                        recv_sem=rsem.at[h, g],
+                        device_id={"ao": target},
+                        device_id_type=MESH,
+                    ).start()
 
     loads[6].wait()
     virt[...] = masked_density(virt[...], masks[2], own_row)
@@ -117,21 +115,23 @@
             for i in range(2):
                 tall[h, pl.ds(2 * k + i, NA, stride=W), :] = other[:, i * HALF : (i + 1) * HALF]
 
-    def turn(ty, _):
+    def turn(i, _):
         for h in range(SLABS):
             for tx in range(X):
-                rows = pl.multiple_of((tx * Y + ty) * (C * W * W), C * W * W)
-                block = tall[h, pl.ds(rows, C * W * W), :]
-                wide[ty, h * HALF : (h + 1) * HALF, tx * C * W * W : (tx + 1) * C * W * W] = block.T.astype(BF16)
+                rows = pl.multiple_of((tx * Y + C * i) * (C * W * W), C * C * W * W)
+                block = tall[h, pl.ds(rows, C * C * W * W), :].T.astype(BF16)
+                for tc in range(C):
+                    mine = [block[:, (C * j + tc) * W * W : (C * j + tc + 1) * W * W] for j in range(C)]
+                    wide[tx * C + tc, h * HALF : (h + 1) * HALF, pl.ds(pl.multiple_of(i * HALF, HALF), HALF)] = jnp.concatenate(mine, axis=1)
         return 0
 
-    lax.fori_loop(0, Y, turn, 0)
+    lax.fori_loop(0, Y // C, turn, 0)
 
     chip = x * Y + y
 
-    def chip_sum(h):
+    def mate_copy(h):
         part = pl.ds(h * CHIPS // SLABS, CHIPS // SLABS)
-        copy = pltpu.make_async_remote_copy(
+        return pltpu.make_async_remote_copy(
             src_ref=psnd.at[1 - c, part],
             dst_ref=pmate.at[part],
             send_sem=mate_send.at[h],
@@ -139,10 +139,12 @@
             device_id={"ao": me + 1 - 2 * c},
             device_id_type=MESH,
         )
-        copy.start()
-        copy.wait_recv()
+
+    def chip_sum(h):
+        part = pl.ds(h * CHIPS // SLABS, CHIPS // SLABS)
+        mate_copy(h).wait_recv()
         psum[part] = psnd[c, part] + pmate[part]
-        return copy
+        plane_send(h)
 
     def plane_send(h):
         for dy in FAR_Y:
@@ -175,30 +177,26 @@
                 device_id_type=MESH,
             ).start()
 
-    mates = []
     for h in range(SLABS):
         total = jnp.zeros((NP, HALF), F32)
-        for step, dy in enumerate((0, 1, 7, 2, 6, 3, 5, 4)):
-            sy = lax.rem(y + Y - dy, Y)
-            pltpu.make_async_copy(rcv.at[h, sy], rcv.at[h, sy], rsem.at[h, dy]).wait()
-            total += dot(wide[sy], rcv[h, sy].reshape(X * C * W * W, HALF))
-            if h == 1 and step == EARLY_SEND:
-                plane_send(0)
-            if h == 1 and step == EARLY_SUM:
-                pl.when(x < X // 2)(window_sum)
+        for g, (dx, dc) in enumerate(SETS):
+            source = lax.rem(x + X - dx, X) * C + lax.rem(c + dc, C)
+            pltpu.make_async_copy(rcv.at[h, source], rcv.at[h, source], rsem.at[h, g]).wait()
+            total += dot(wide[source], rcv[h, source].reshape(Y * W * W, HALF))
+            if h == 1 and g == EARLY_SEND:
+                chip_sum(0)
         low = total[:HALF].T.reshape(CHIPS // SLABS, 8, HALF)
         high = total[HALF:].T.reshape(CHIPS // SLABS, 8, HALF)
         top = lax.broadcasted_iota(jnp.int32, low.shape, 1) < 4
         part = pl.ds(h * CHIPS // SLABS, CHIPS // SLABS)
         psnd[0, part] = jnp.where(top, low, pltpu.roll(high, 4, 1))
         psnd[1, part] = jnp.where(top, pltpu.roll(low, 4, 1), high)
-        mates.append(chip_sum(h))
-
-    plane_send(1)
-    if EARLY_SUM < 0:
-        window_sum()
-    else:
-        pl.when(x >= X // 2)(window_sum)
+        mate_copy(h).start()
+
+    if EARLY_SEND == len(SETS):
+        chip_sum(0)
+    chip_sum(1)
+    window_sum()
     pltpu.make_async_copy(zrcv.at[pl.ds(0, Z - 1)], zrcv.at[pl.ds(0, Z - 1)], zsem).wait()
     total = jnp.sum(zrcv[...], axis=0)
     out_ref[:, 0:HALF] = total[0:4]
@@ -206,8 +204,8 @@
 
     for h in range(SLABS):
         pltpu.make_async_copy(snd.at[h, pl.ds(0, AO - 1)], snd.at[h, pl.ds(0, AO - 1)], ssem.at[h]).wait()
-    for mate in mates:
-        mate.wait_send()
+    for h in range(SLABS):
+        mate_copy(h).wait_send()
     pltpu.make_async_copy(prcv.at[pl.ds(0, CHIPS - 1)], prcv.at[pl.ds(0, CHIPS - 1)], psend_sem).wait()
     pltpu.make_async_copy(zrcv.at[pl.ds(0, Z - 1)], zrcv.at[pl.ds(0, Z - 1)], zsend_sem).wait()
 
@@ -229,16 +227,16 @@
             pltpu.VMEM((NA * W, HALF), F32),
             pltpu.VMEM((SLABS, W // 2, NA, 2 * HALF), BF16),
             pltpu.VMEM((SLABS, AO, W * W, HALF), BF16),
-            pltpu.VMEM((SLABS, Y, X * C, W * W, HALF), BF16),
+            pltpu.VMEM((SLABS, X * C, Y, W * W, HALF), BF16),
             pltpu.VMEM((SLABS, NA * W, HALF), F32),
-            pltpu.VMEM((Y, NP, X * C * W * W), BF16),
+            pltpu.VMEM((X * C, NP, Y * W * W), BF16),
             pltpu.VMEM((C, CHIPS, 8, HALF), F32),
             pltpu.VMEM((CHIPS, 8, HALF), F32),
             pltpu.VMEM((CHIPS, 8, HALF), F32),
             pltpu.VMEM((CHIPS, 8, HALF), F32),
             pltpu.VMEM((8, HALF), F32),
             pltpu.VMEM((Z, 8, HALF), F32),
-            dma((7,)), dma((SLABS,)), dma((SLABS, Y)), dma((SLABS,)), dma((SLABS,)), dma, dma, dma, dma,
+            dma((7,)), dma((SLABS,)), dma((SLABS, len(SETS))), dma((SLABS,)), dma((SLABS,)), dma, dma, dma, dma,
         ],
         compiler_params=pltpu.CompilerParams(
             collective_id=0, has_side_effects=True, vmem_limit_bytes=60 * 2**20

time: 81.7 us -> 81.5 us (level)
  no operation moved by 1% of the time
where the time goes in v3:
time: 81.5 us; the launch traced here: 81.3 us
  Pallas kernels  80 us (98%)
  local copies, waits for them, and re-layouts  1.28 us (2%)
    pallas_call x1, Pallas kernels, body(): pl.pallas_call(kernel, out_shape=jax.ShapeDtypeStruct((NP // AO, NP), F32...  80 us

profile of v3, /device:TPU:6, one launch (start us, length us, event | category | flops | bytes accessed | tf_op | source)
XLA Modules:
  0.0 81.3 jit_solution(14717061117785171382)
XLA Ops:
  0.0 80.0 %response.1 = f32[4,256]{1,0:T(4,128)} custom-call(bf16[1,512,8,256]{3,2,1,0:T(8,128)(2,1)} %three_hbm.1, bf16[1,512,512]{2,1,0:T(8,128)(2,1)} %occ_hbm.1, bf16[1,512,512]{2,1,0:T(8,128)(2,1)} %virt_hbm.1, s32[1,16,16]{2,1,0:T(8,128)} %pair_hbm.1, s32[1,16,16]{2,1,0:T(8,128)} %occ_mask_hbm.1, s32[1,16,16]{2,1,0:T(8,128)} %virt_mask_hbm.1), custom_call_target="tpu_custom_call" | custom-call | tf_op jit(solution)/shard_map/response/pallas_call | solution.py:217
  80.0 1.3 %copy.8 = f32[4,256]{1,0:T(4,128)} copy(f32[4,256]{1,0:T(4,128)} %response.1) | data formatting | bytes 8192
